TPU v7x, 32 devices: a whole 2x2x4 slice. The times are simulated.
32 devices in a mesh: dp: 8 (over y, x, core), tensor: 4 (over z).
Axes of the slice: x: 2, y: 2, z: 4, core: 2. Of those that a mesh axis runs over, the one named last changes fastest.
Arguments:
- hidden: bfloat16 [1024, 8192], P('dp', 'tensor')
- rotation: float32 [8192, 8192], P('dp', 'tensor'), may hold values from -0.0625 to 0.0625
- channel_scale: float32 [8192], P('tensor')
- lengths: int32 [16], P('dp'), may hold values from 16 to 64, as said below
Outputs:
- direction: float32 [8192, 8192], P('dp', 'tensor')
- loss: float32 [], replicated
Inputs may be any that keep to these rules, and one draw needn't show every extreme that they name: `lengths`: each sequence's valid length; some sequence is full in every draw.
All inputs are finite; a program needn't handle non-finite values.
Results may differ from a plain program's by a relative error of at most 0.00075.
The roundings to bfloat16 on the way count: a program that leaves them out, or rounds other values in their place, can miss the bound.
Values may be sent and summed in bfloat16 or wider, within the bound.
A program may use at most 128 MiB of HBM per device.

v0:
```python
import math

import jax
import jax.numpy as jnp
from jax import lax
from jax.sharding import PartitionSpec as P

D = 8192
SEQ = 64


def local(hidden, rotation, channel_scale, lengths):
    narrow_rotation = rotation.astype(jnp.bfloat16)
    features = lax.all_gather(hidden, "tensor", axis=1, tiled=True)
    column_blocks = lax.all_to_all(features, "dp", split_axis=1, concat_axis=0, tiled=True)
    rotated = jnp.dot(
        features,
        lax.all_gather(narrow_rotation, "dp", axis=0, tiled=True),
        preferred_element_type=jnp.float32,
    )
    scaled = rotated * channel_scale[None, :]
    token_square = lax.psum(jnp.sum(scaled * scaled, axis=1), "tensor")
    step_size = 4.0 * jnp.sqrt(token_square / D + 1e-06)[:, None]
    token_index = jnp.arange(hidden.shape[0], dtype=jnp.int32)
    position = token_index % SEQ
    sequence_index = token_index // SEQ
    sequence_count = lengths.shape[0]
    owners = sequence_index[:, None] == jnp.arange(sequence_count, dtype=jnp.int32)[None, :]
    inside = position[:, None] < lengths[None, :]
    live_mask = jnp.sum(jnp.where(owners & inside, 1.0, 0.0), axis=1).astype(jnp.float32)[:, None]
    angles = math.pi * scaled / step_size
    error_local = jnp.sum(live_mask * jnp.sin(angles) ** 2)
    count_local = jnp.sum(lengths).astype(jnp.float32) / lax.axis_size("tensor")
    error_slope = (
        live_mask * (math.pi / step_size) * jnp.sin(2.0 * angles) * channel_scale[None, :]
    ).astype(jnp.bfloat16)
    gradient = lax.dot_general(
        column_blocks,
        lax.all_gather(error_slope, "dp", axis=0, tiled=True),
        (((0,), (0,)), ((), ())),
        preferred_element_type=jnp.float32,
    )
    error_sum, count = lax.psum((error_local, count_local), ("dp", "tensor"))
    grad_square = lax.psum(jnp.sum(gradient * gradient), ("dp", "tensor"))
    direction = gradient / jnp.sqrt(grad_square / (D * D) + 1e-06)
    loss = error_sum / (D * count)
    return (direction, loss)


def solution(mesh):
    return jax.shard_map(
        local,
        mesh=mesh,
        in_specs=(P("dp", "tensor"), P("dp", "tensor"), P("tensor"), P("dp")),
        out_specs=(P("dp", "tensor"), P()),
        check_vma=False,
    )
```

profile of v0, /device:TPU:0, one launch (start us, length us, event | category | flops | bytes accessed | tf_op | source)
XLA Modules:
  0.0 379.5 jit_solution(14552061556022598710)
XLA Ops:
  7.2 0.0 all-gather.4.cloned.1.call-start
  7.2 2.1 copy.11
  9.3 0.0 all-gather.4.cloned.1.call-update
  9.3 0.0 all-gather.6.cloned.1.call-start
  9.3 6.1 %convert_element_type.9 = bf16[1024,2048]{1,0:T(8,128)(2,1)} convert(f32[1024,2048]{1,0:T(8,128)} %param.5) | non-fusion elementwise | flops 2097152 | bytes 12582912 | tf_op jit(solution)/shard_map/convert_element_type | solution.py:13
  15.4 0.0 copy-start.1
  15.4 0.0 copy-start
  15.4 0.0 all-gather.6.cloned.1.call-update
  15.4 0.0 all-gather.8.cloned.1.call-start
  15.5 0.6 copy-done.1
  16.1 0.1 fusion
  16.1 42.1 %all-gather.4.cloned.1.call-done = bf16[128,8192]{0,1:T(8,128)(2,1)} async-done(((bf16[128,2048]{0,1:T(8,128)(2,1)}), bf16[128,8192]{0,1:T(8,128)(2,1)}) %all-gather.4.cloned.1.call-update) | async-done | bytes 2097168 | tf_op jit(solution)/shard_map/all_gather | solution.py:14
  58.2 162.0 %all-gather.6.cloned.1.call-done = bf16[8192,2048]{1,0:T(8,128)(2,1)} async-done(((bf16[1024,2048]{1,0:T(8,128)(2,1)}), bf16[8192,2048]{1,0:T(8,128)(2,1)}) %all-gather.6.cloned.1.call-update) | async-done | bytes 33554448 | tf_op jit(solution)/shard_map/all_gather | solution.py:18
  220.2 0.0 copy-done
  220.2 13.6 %multiply_reduce_fusion.2 = (f32[128]{0:T(128)S(1)}, f32[128,2048]{1,0:T(8,128)S(1)}) fusion(f32[2048]{0:T(1024)S(1)} %copy-done, bf16[128,8192]{0,1:T(8,128)(2,1)} %all-gather.4.cloned.1.call-done, bf16[8192,2048]{1,0:T(8,128)(2,1)} %all-gather.6.cloned.1.call-done), kind=kOutput, calls=%fused_computation.6 | convolution fusion | flops 4295753728 | bytes 36708864 | tf_op jit(solution)/shard_map/dot_general | solution.py:16
  233.8 11.7 %psum.28 = f32[128]{0:T(128)S(1)} all-reduce(f32[128]{0:T(128)S(1)} %get-tuple-element.17), channel_id=1, replica_groups=mesh['dp'=8,'tensor'=4] {'tensor'}, use_global_device_ids=true, to_apply=%region_2.3 | all-reduce | flops 128 | bytes 1024 | tf_op jit(solution)/shard_map/psum | solution.py:22
  245.5 8.6 %multiply_reduce_fusion.1 = (f32[]{:T(128)}, bf16[128,2048]{1,0:T(8,128)(2,1)}) fusion(f32[128]{0:T(128)S(1)} %fusion, f32[128]{0:T(128)S(1)} %get-tuple-element.15, f32[128,2048]{1,0:T(8,128)S(1)} %get-tuple-element.18, f32[2048]{0:T(1024)S(1)} %copy-done, f32[128]{0:T(128)S(1)} %get-tuple-element.16), kind=kLoop, calls=%fused_computation.3 | loop fusion | flops 2359295 | bytes 1582596 | tf_op jit(solution)/shard_map/reduce_sum | solution.py:32
  254.1 0.0 all-gather.8.cloned.1.call-update
  254.1 3.6 all-to-all-start
  257.7 0.6 reduce_sum.49
  259.0 31.9 %all-to-all-done = bf16[128,8,1024]{0,2,1:T(8,128)(2,1)S(1)} async-done(((bf16[128,8,1024]{0,2,1:T(8,128)(2,1)}), bf16[128,8,1024]{0,2,1:T(8,128)(2,1)S(1)}, u32[]{:S(2)}, u32[]{:S(2)}) %all-to-all-start) | async-done | bytes 2097184 | tf_op jit(solution)/shard_map/all_to_all | solution.py:15
  290.9 2.6 copy.12
  293.5 9.4 %all-gather.8.cloned.1.call-done = bf16[1024,2048]{1,0:T(8,128)(2,1)} async-done(((bf16[128,2048]{1,0:T(8,128)(2,1)}), bf16[1024,2048]{1,0:T(8,128)(2,1)}) %all-gather.8.cloned.1.call-update) | async-done | bytes 4194320 | tf_op jit(solution)/shard_map/all_gather | solution.py:39
  302.9 11.4 %multiply_reduce_fusion = (f32[]{:T(128)}, f32[2048,1024]{1,0:T(8,128)}) fusion(bf16[1024,2048]{1,0:T(8,128)(2,1)} %all-gather.8.cloned.1.call-done, bf16[1024,1024]{1,0:T(8,128)(2,1)} %bitcast.10), kind=kOutput, calls=%fused_computation.1 | convolution fusion | flops 4299161600 | bytes 14680068 | tf_op jit(solution)/shard_map/dot_general | solution.py:37
  314.3 38.0 %all-reduce = (f32[]{:T(128)}, f32[]{:T(128)}, f32[]{:T(128)}) all-reduce(f32[]{:T(128)} %get-tuple-element.19, f32[]{:T(128)} %get-tuple-element.13, f32[]{:T(128)S(6)} %div.59), channel_id=1, replica_groups=mesh['dp'=8,'tensor'=4] {'dp','tensor'}, use_global_device_ids=true, to_apply=%region_4.5 | all-reduce | flops 3 | bytes 24 | tf_op jit(solution)/shard_map/psum | solution.py:44
  353.0 8.5 %divide_bitcast_fusion = f32[1024,2048]{0,1:T(8,128)} fusion(f32[2048,1024]{1,0:T(8,128)} %get-tuple-element.20, f32[]{:T(128)S(6)} %sqrt.7), kind=kLoop, calls=%fused_computation | loop fusion | flops 2097152 | bytes 16777220 | tf_op jit(solution)/shard_map/div | solution.py:45
  361.5 9.1 %copy.13 = f32[1024,2048]{1,0:T(8,128)} copy(f32[1024,2048]{0,1:T(8,128)} %divide_bitcast_fusion) | data formatting | bytes 16777216
  (2 shorter events, 0.0 us)
Async XLA Ops:
  7.2 51.1 %all-gather.4.cloned.1.call-start = ((), (), s32[]{:S(2)}) async-start(), calls=%async_computation.1 | async-start | bytes 2621440 | tf_op jit(solution)/shard_map/all_gather | solution.py:14
  9.3 210.9 %all-gather.6.cloned.1.call-start = ((), (), s32[]{:S(2)}) async-start(), calls=%async_computation.2 | async-start | bytes 37748736 | tf_op jit(solution)/shard_map/all_gather | solution.py:18
  15.4 0.7 copy-start.1
  15.4 204.8 %copy-start = (f32[2048]{0:T(1024)S(1)}, f32[2048]{0:T(1024)}, u32[]{:S(2)}) copy-start(f32[2048]{0:T(1024)} %param.6) | copy-start | bytes 24580
  15.4 287.4 %all-gather.8.cloned.1.call-start = ((), (), s32[]{:S(2)}) async-start(), calls=%async_computation.3 | async-start | bytes 4718592 | tf_op jit(solution)/shard_map/all_gather | solution.py:39
  254.1 36.8 %all-to-all-start = ((bf16[128,8,1024]{0,2,1:T(8,128)(2,1)}), bf16[128,8,1024]{0,2,1:T(8,128)(2,1)S(1)}, u32[]{:S(2)}, u32[]{:S(2)}) async-start(bf16[128,8,1024]{0,2,1:T(8,128)(2,1)} %bitcast), calls=%async_computation | async-start | bytes 4194304 | tf_op jit(solution)/shard_map/all_to_all | solution.py:15
Sparse Core Ops, SparseCore 0:
  9.6 48.6 all-gather.3
  60.7 159.4 all-gather.5
  254.2 48.5 all-gather.7
where the time goes:
time: 380 us; the launch traced here: 379 us
  waiting for transfers between devices  245 us (64%)
  blocking collectives  49.7 us (13%)
  matrix products  25 us (7%)
  other arithmetic  23.9 us (6%)
  between operations  17.4 us (5%)
  local copies, waits for them, and re-layouts  14.4 us (4%)
    all_gather x1, waiting for transfers between devices, local(): lax.all_gather(narrow_rotation, 'dp', axis=0, tiled=True)  162 us
    all_gather x1, waiting for transfers between devices, local(): features = lax.all_gather(hidden, 'tensor', axis=1, tiled=True)  42.1 us
    psum x1, blocking collectives, local(): grad_square = lax.psum(jnp.sum(gradient * gradient), ('dp', 'tensor'))  38 us
    all_to_all x1, waiting for transfers between devices, local(): lax.all_to_all(features, 'dp', split_axis=1, concat_axis=0, tiled=True)  31.9 us
    dot_general x1, matrix products, local(): jnp.dot(features, lax.all_gather(narrow_rotation, 'dp', axis=0, tiled=Tru...  13.6 us
    unnamed x6, local copies, waits for them, and re-layouts  11.8 us
    psum x1, blocking collectives, local(): token_square = lax.psum(jnp.sum(scaled * scaled, axis=1), 'tensor')  11.7 us
    dot_general x1, matrix products, local(): lax.dot_general(column_blocks, lax.all_gather(error_slope, 'dp', axis=0,...  11.4 us
  transfers between devices with their start and end apart: 4, of which 4 were waited for; matrix products, arithmetic and copies ran while one was open for 2% of the time, Pallas kernels for 0%

commit v1 on v0

--- a/solution.py
+++ b/solution.py
@@ -13,11 +13,8 @@
     narrow_rotation = rotation.astype(jnp.bfloat16)
     features = lax.all_gather(hidden, "tensor", axis=1, tiled=True)
     column_blocks = lax.all_to_all(features, "dp", split_axis=1, concat_axis=0, tiled=True)
-    rotated = jnp.dot(
-        features,
-        lax.all_gather(narrow_rotation, "dp", axis=0, tiled=True),
-        preferred_element_type=jnp.float32,
-    )
+    partial = jnp.dot(column_blocks, narrow_rotation, preferred_element_type=jnp.float32)
+    rotated = lax.psum_scatter(partial, "dp", scatter_dimension=0, tiled=True)
     scaled = rotated * channel_scale[None, :]
     token_square = lax.psum(jnp.sum(scaled * scaled, axis=1), "tensor")
     step_size = 4.0 * jnp.sqrt(token_square / D + 1e-06)[:, None]

time: 380 us -> 307 us (0.81)
  waiting for transfers between devices: 245 us -> 150 us
  blocking collectives: 49.7 us -> 81.5 us
    all_gather x1 -> x0, waiting for transfers between devices: 162 us -> none  [local(): lax.all_gather(narrow_rotation, 'dp', axis=0, tiled=True)]
    reduce_scatter x0 -> x1, waiting for transfers between devices: none -> 67.6 us  [local(): rotated = lax.psum_scatter(partial, 'dp', scatter_dimension=0, tiled=True)]
    all_to_all x1 -> x0, waiting for transfers between devices: 31.9 us -> none  [local(): lax.all_to_all(features, 'dp', split_axis=1, concat_axis=0, tiled=True)]
    all_to_all x0 -> x1, blocking collectives: none -> 30.2 us  [local(): lax.all_to_all(features, 'dp', split_axis=1, concat_axis=0, tiled=True)]
    all_gather x1, waiting for transfers between devices: 9.35 us -> 32.9 us  [local(): lax.all_gather(error_slope, 'dp', axis=0, tiled=True)]
    all_gather x1, waiting for transfers between devices: 42.1 us -> 49.5 us  [local(): features = lax.all_gather(hidden, 'tensor', axis=1, tiled=True)]
    convert_element_type x1 -> x0, other arithmetic: 6.05 us -> none  [local(): narrow_rotation = rotation.astype(jnp.bfloat16)]
    unnamed x6 -> x8, local copies, waits for them, and re-layouts: 11.8 us -> 11.7 us
  transfers between devices with their start and end apart: 4 -> 3, of which waited for: 4 -> 3; matrix products, arithmetic and copies ran while one was open for 2% -> 0% of each run, Pallas kernels for 0% -> 0%
where the time goes in v1:
time: 307 us; the launch traced here: 306 us
  waiting for transfers between devices  150 us (49%)
  blocking collectives  81.5 us (27%)
  matrix products  22 us (7%)
  other arithmetic  20.6 us (7%)
  between operations  17.3 us (6%)
  local copies, waits for them, and re-layouts  14.3 us (5%)
    reduce_scatter x1, waiting for transfers between devices, local(): rotated = lax.psum_scatter(partial, 'dp', scatter_dimension=0, tiled=True)  67.6 us
    all_gather x1, waiting for transfers between devices, local(): features = lax.all_gather(hidden, 'tensor', axis=1, tiled=True)  49.5 us
    psum x1, blocking collectives, local(): grad_square = lax.psum(jnp.sum(gradient * gradient), ('dp', 'tensor'))  39.6 us
    all_gather x1, waiting for transfers between devices, local(): lax.all_gather(error_slope, 'dp', axis=0, tiled=True)  32.9 us
    all_to_all x1, blocking collectives, local(): lax.all_to_all(features, 'dp', split_axis=1, concat_axis=0, tiled=True)  30.2 us
    dot_general x1, matrix products, local(): jnp.dot(column_blocks, narrow_rotation, preferred_element_type=jnp.float32)  11.9 us
    unnamed x8, local copies, waits for them, and re-layouts  11.7 us
    psum x1, blocking collectives, local(): token_square = lax.psum(jnp.sum(scaled * scaled, axis=1), 'tensor')  11.7 us
  transfers between devices with their start and end apart: 3, of which 3 were waited for; matrix products, arithmetic and copies ran while one was open for 0% of the time, Pallas kernels for 0%

profile of v1, /device:TPU:0, one launch (start us, length us, event | category | flops | bytes accessed | tf_op | source)
XLA Modules:
  0.0 305.9 jit_solution(8076852472374651479)
XLA Ops:
  7.2 0.0 all-gather.3.cloned.1.call-start
  7.2 2.0 copy.11
  9.3 0.0 all-gather.3.cloned.1.call-update
  9.3 0.0 reduce-scatter.2.cloned.1.call-start
  9.3 49.5 %all-gather.3.cloned.1.call-done = bf16[128,8192]{0,1:T(8,128)(2,1)} async-done(((bf16[128,2048]{0,1:T(8,128)(2,1)}), bf16[128,8192]{0,1:T(8,128)(2,1)}) %all-gather.3.cloned.1.call-update) | async-done | bytes 2097168 | tf_op jit(solution)/shard_map/all_gather | solution.py:14
  58.8 30.2 %all_to_all.19 = bf16[128,8,1024]{0,2,1:T(8,128)(2,1)S(1)} all-to-all(bf16[128,8,1024]{0,2,1:T(8,128)(2,1)} %bitcast.11), channel_id=1, replica_groups=mesh['dp'=8,'tensor'=4] {'dp'}, dimensions={1} | all-to-all | bytes 4194304 | tf_op jit(solution)/shard_map/all_to_all | solution.py:15
  89.0 2.6 copy.12
  91.6 11.9 %fusion = f32[1024,2048]{1,0:T(8,128)} fusion(bf16[1024,1024]{1,0:T(8,128)(2,1)} %bitcast.9, f32[1024,2048]{1,0:T(8,128)} %param.5), kind=kOutput, calls=%fused_computation.2 | convolution fusion | flops 4297064448 | bytes 18874368 | tf_op jit(solution)/shard_map/dot_general | solution.py:16
  103.6 0.0 copy-start.2
  103.6 0.0 copy-start.1
  103.6 0.0 copy-start
  103.6 0.0 reduce-scatter.2.cloned.1.call-update
  103.6 0.0 all-gather.5.cloned.1.call-start
  103.6 0.6 copy-done.2
  104.2 0.1 fusion.2
  104.3 67.6 %reduce-scatter.2.cloned.1.call-done = f32[128,2048]{1,0:T(8,128)} async-done(((f32[1024,2048]{1,0:T(8,128)}), f32[128,2048]{1,0:T(8,128)}) %reduce-scatter.2.cloned.1.call-update) | async-done | bytes 1048592 | tf_op jit(solution)/shard_map/reduce_scatter | solution.py:17
  171.9 0.0 copy-done.1
  171.9 1.4 multiply_reduce_fusion.2
  173.3 11.7 %psum.28 = f32[128]{0:T(128)S(1)} all-reduce(f32[128]{0:T(128)S(1)} %multiply_reduce_fusion.2), channel_id=1, replica_groups=mesh['dp'=8,'tensor'=4] {'tensor'}, use_global_device_ids=true, to_apply=%region_3.4 | all-reduce | flops 128 | bytes 1024 | tf_op jit(solution)/shard_map/psum | solution.py:19
  185.0 9.9 %multiply_reduce_fusion.1 = (f32[]{:T(128)}, bf16[128,2048]{1,0:T(8,128)(2,1)}) fusion(f32[128]{0:T(128)S(1)} %fusion.2, f32[128]{0:T(128)S(1)} %get-tuple-element.15, f32[128,2048]{1,0:T(8,128)} %reduce-scatter.2.cloned.1.call-done, f32[2048]{0:T(1024)S(1)} %copy-done.1, f32[128]{0:T(128)S(1)} %get-tuple-element.16), kind=kLoop, calls=%fused_computation.4 | loop fusion | flops 2621439 | bytes 1582596 | tf_op jit(solution)/shard_map/reduce_sum | solution.py:29
  194.9 0.0 all-gather.5.cloned.1.call-update
  195.0 0.6 reduce_sum.49
  196.2 32.9 %all-gather.5.cloned.1.call-done = bf16[1024,2048]{1,0:T(8,128)(2,1)} async-done(((bf16[128,2048]{1,0:T(8,128)(2,1)}), bf16[1024,2048]{1,0:T(8,128)(2,1)}) %all-gather.5.cloned.1.call-update) | async-done | bytes 4194320 | tf_op jit(solution)/shard_map/all_gather | solution.py:36
  229.0 0.0 copy-done
  229.1 10.1 %multiply_reduce_fusion = (f32[]{:T(128)}, f32[2048,1024]{1,0:T(8,128)}) fusion(bf16[1024,2048]{1,0:T(8,128)(2,1)} %all-gather.5.cloned.1.call-done, bf16[1024,1024]{1,0:T(8,128)(2,1)S(1)} %bitcast.10), kind=kOutput, calls=%fused_computation.1 | convolution fusion | flops 4299161600 | bytes 14680068 | tf_op jit(solution)/shard_map/dot_general | solution.py:34
  239.2 39.6 %all-reduce = (f32[]{:T(128)}, f32[]{:T(128)}, f32[]{:T(128)}) all-reduce(f32[]{:T(128)} %get-tuple-element.17, f32[]{:T(128)} %get-tuple-element.13, f32[]{:T(128)S(6)} %div.59), channel_id=1, replica_groups=mesh['dp'=8,'tensor'=4] {'dp','tensor'}, use_global_device_ids=true, to_apply=%region_5.6 | all-reduce | flops 3 | bytes 24 | tf_op jit(solution)/shard_map/psum | solution.py:41
  279.4 8.5 %divide_bitcast_fusion = f32[1024,2048]{0,1:T(8,128)} fusion(f32[2048,1024]{1,0:T(8,128)} %get-tuple-element.18, f32[]{:T(128)S(6)} %sqrt.7), kind=kLoop, calls=%fused_computation | loop fusion | flops 2097152 | bytes 16777220 | tf_op jit(solution)/shard_map/div | solution.py:42
  287.9 9.1 %copy.13 = f32[1024,2048]{1,0:T(8,128)} copy(f32[1024,2048]{0,1:T(8,128)} %divide_bitcast_fusion) | data formatting | bytes 16777216
  (2 shorter events, 0.0 us)
Async XLA Ops:
  7.2 51.6 %all-gather.3.cloned.1.call-start = ((), (), s32[]{:S(2)}) async-start(), calls=%async_computation.2 | async-start | bytes 2621440 | tf_op jit(solution)/shard_map/all_gather | solution.py:14
  9.3 162.6 %reduce-scatter.2.cloned.1.call-start = ((), (), s32[]{:S(2)}) async-start(), calls=%async_computation.3 | async-start | bytes 9437184 | tf_op jit(solution)/shard_map/reduce_scatter | solution.py:17
  103.6 0.7 copy-start.2
  103.6 68.4 %copy-start.1 = (f32[2048]{0:T(1024)S(1)}, f32[2048]{0:T(1024)}, u32[]{:S(2)}) copy-start(f32[2048]{0:T(1024)} %param.6) | copy-start | bytes 24580
  103.6 125.5 %copy-start = (bf16[8,128,1024]{2,1,0:T(8,128)(2,1)S(1)}, bf16[8,128,1024]{2,1,0:T(8,128)(2,1)}, u32[]{:S(2)}) copy-start(bf16[8,128,1024]{2,1,0:T(8,128)(2,1)} %copy.12) | copy-start | bytes 6291460
  103.6 125.5 %all-gather.5.cloned.1.call-start = ((), (), s32[]{:S(2)}) async-start(), calls=%async_computation.4 | async-start | bytes 4718592 | tf_op jit(solution)/shard_map/all_gather | solution.py:36
Sparse Core Ops, SparseCore 0:
  10.1 48.6 all-gather.2
  103.7 68.1 reduce-scatter.1
  195.1 33.9 all-gather.4

commit v2 on v1

v2 whole, which is shorter than its diff:
```python
import functools
import math

import jax
import jax.numpy as jnp
from jax import lax
from jax.experimental import pallas as pl
from jax.experimental.pallas import tpu as pltpu
from jax.sharding import PartitionSpec as P

D = 8192
SEQ = 64
MESH = pl.DeviceIdType.MESH


def greet(axes):
    barrier = pltpu.get_barrier_semaphore()
    total = 0
    for axis, n in axes:
        me = lax.axis_index(axis)
        for off in range(1, n):
            pl.semaphore_signal(barrier, inc=1, device_id={axis: lax.rem(me + off, n)}, device_id_type=MESH)
        total += n - 1
    pl.semaphore_wait(barrier, total)


def all_sum(axis, n, slots, send, recv, value):
    me = lax.axis_index(axis)
    slots[me] = value
    copies = []
    for off in range(1, n):
        copy = pltpu.make_async_remote_copy(
            src_ref=slots.at[me],
            dst_ref=slots.at[me],
            send_sem=send.at[off],
            recv_sem=recv.at[off],
            device_id={axis: lax.rem(me + off, n)},
            device_id_type=MESH,
        )
        copy.start()
        copies.append(copy)
    for copy in copies:
        copy.wait()
    return jnp.sum(slots[...], axis=0)


def token_kernel(nt, x_ref, o_ref, slots, send, recv):
    greet([("tensor", nt)])
    o_ref[...] = all_sum("tensor", nt, slots, send, recv, x_ref[...])


def token_sum(nt, x):
    return pl.pallas_call(
        functools.partial(token_kernel, nt),
        out_shape=jax.ShapeDtypeStruct(x.shape, jnp.float32),
        in_specs=[pl.BlockSpec(memory_space=pltpu.VMEM)],
        out_specs=pl.BlockSpec(memory_space=pltpu.VMEM),
        scratch_shapes=[
            pltpu.VMEM((nt,) + x.shape, jnp.float32),
            pltpu.SemaphoreType.DMA((nt,)),
            pltpu.SemaphoreType.DMA((nt,)),
        ],
        compiler_params=pltpu.CompilerParams(collective_id=0, has_side_effects=True),
    )(x)


def gradient_kernel(nd, nt, tile, h_ref, s_ref, extra_ref, g_ref, o_ref, buf, out_sem, tslots, dslots, ts, tr, ds, dr):
    greet([("dp", nd), ("tensor", nt)])
    rows, columns = g_ref.shape
    steps = columns // tile
    square = jnp.zeros((8, tile), jnp.float32)
    copies = []
    for step in range(steps):
        slot = step % 2
        if step >= 2:
            copies[step - 2].wait()
        block = jnp.dot(h_ref[...], s_ref[:, step * tile:(step + 1) * tile], preferred_element_type=jnp.float32)
        buf[slot] = block
        square = square + jnp.sum((block * block).reshape(rows // 8, 8, tile), axis=0)
        copy = pltpu.make_async_copy(buf.at[slot], g_ref.at[:, pl.ds(step * tile, tile)], out_sem.at[slot])
        copy.start()
        copies.append(copy)
    row = lax.broadcasted_iota(jnp.int32, (8, 128), 0)
    value = extra_ref[...] + jnp.where(row == 0, jnp.sum(square), 0.0)
    value = all_sum("tensor", nt, tslots, ts, tr, value)
    o_ref[...] = all_sum("dp", nd, dslots, ds, dr, value)
    for copy in copies[-2:]:
        copy.wait()


def gradient_call(nd, nt, h, s, extra):
    rows, columns = h.shape[0], s.shape[1]
    tile = 256
    vmem = pl.BlockSpec(memory_space=pltpu.VMEM)
    dma = pltpu.SemaphoreType.DMA
    return pl.pallas_call(
        functools.partial(gradient_kernel, nd, nt, tile),
        out_shape=(
            jax.ShapeDtypeStruct((rows, columns), jnp.float32),
            jax.ShapeDtypeStruct((8, 128), jnp.float32),
        ),
        in_specs=[vmem, vmem, vmem],
        out_specs=(pl.BlockSpec(memory_space=pl.ANY), vmem),
        scratch_shapes=[
            pltpu.VMEM((2, rows, tile), jnp.float32),
            dma((2,)),
            pltpu.VMEM((nt, 8, 128), jnp.float32),
            pltpu.VMEM((nd, 8, 128), jnp.float32),
            dma((nt,)),
            dma((nt,)),
            dma((nd,)),
            dma((nd,)),
        ],
        compiler_params=pltpu.CompilerParams(
            collective_id=1, has_side_effects=True, vmem_limit_bytes=40 * 1024 * 1024
        ),
    )(h, s, extra)


def sin_cos_pi(turns):
    v = turns - jnp.round(turns)
    x = math.pi * v
    z = x * x
    s = x * (1.0 + z * (-1 / 6 + z * (1 / 120 + z * (-1 / 5040 + z * (1 / 362880 - z * (1 / 39916800))))))
    c = 1.0 + z * (-0.5 + z * (1 / 24 + z * (-1 / 720 + z * (1 / 40320 + z * (-1 / 3628800 + z * (1 / 479001600))))))
    return s, c


def local(hidden, rotation, channel_scale, lengths):
    nd, nt = lax.axis_size("dp"), lax.axis_size("tensor")
    tokens = hidden.shape[0]
    narrow_rotation = rotation.astype(jnp.bfloat16)
    features = lax.all_gather(hidden, "tensor", axis=1, tiled=True)
    column_blocks = lax.all_to_all(features, "dp", split_axis=1, concat_axis=0, tiled=True)
    partial = jnp.dot(column_blocks, narrow_rotation, preferred_element_type=jnp.float32)
    rotated = lax.psum_scatter(partial, "dp", scatter_dimension=0, tiled=True)
    scaled = rotated * channel_scale[None, :]
    own_square = jnp.sum(scaled * scaled, axis=1)
    token_square = token_sum(nt, jnp.broadcast_to(own_square[None, :], (8, tokens)))[0]
    step_size = 4.0 * jnp.sqrt(token_square / D + 1e-06)[:, None]
    token_index = jnp.arange(tokens, dtype=jnp.int32)
    position = token_index % SEQ
    sequence_index = token_index // SEQ
    sequence_count = lengths.shape[0]
    owners = sequence_index[:, None] == jnp.arange(sequence_count, dtype=jnp.int32)[None, :]
    inside = position[:, None] < lengths[None, :]
    live_mask = jnp.sum(jnp.where(owners & inside, 1.0, 0.0), axis=1).astype(jnp.float32)[:, None]
    sine, cosine = sin_cos_pi(scaled / step_size)
    error_local = jnp.sum(live_mask * sine * sine)
    count_local = jnp.sum(lengths).astype(jnp.float32) / nt
    error_slope = (
        live_mask * (math.pi / step_size) * (2.0 * sine * cosine) * channel_scale[None, :]
    ).astype(jnp.bfloat16)
    slopes = lax.all_gather(error_slope, "dp", axis=0, tiled=True)
    row = lax.broadcasted_iota(jnp.int32, (8, 128), 0)
    extra = jnp.where(row == 1, error_local, jnp.where(row == 2, count_local, 0.0))
    gradient, totals = gradient_call(nd, nt, column_blocks.T, slopes, extra)
    direction = gradient * (1.0 / jnp.sqrt(totals[0, 0] / (D * D) + 1e-06))
    loss = totals[1, 0] / (D * totals[2, 0])
    return (direction, loss)


def solution(mesh):
    return jax.shard_map(
        local,
        mesh=mesh,
        in_specs=(P("dp", "tensor"), P("dp", "tensor"), P("tensor"), P("dp")),
        out_specs=(P("dp", "tensor"), P()),
        check_vma=False,
    )
```

time: 307 us -> 263 us (0.86)
  blocking collectives: 81.5 us -> 30 us
  Pallas kernels: 0 us -> 26.5 us
  matrix products: 22 us -> 10.2 us
  other arithmetic: 20.6 us -> 15.9 us
  local copies, waits for them, and re-layouts: 14.3 us -> 10.3 us
    psum x2 -> x0, blocking collectives: 51.3 us -> none  [the longest x1 39.6 us: local(): grad_square = lax.psum(jnp.sum(gradient * gradient), ('dp', 'tensor'))]
    pallas_call x0 -> x2, Pallas kernels: none -> 26.5 us  [the longest x1 19.7 us: gradient_call(): pl.pallas_call(functools.partial(gradient_kernel, nd, nt, tile), out_shap...]
    dot_general x1 -> x0, matrix products: 10.1 us -> none  [local(): lax.dot_general(column_blocks, lax.all_gather(error_slope, 'dp', axis=0,...]
    mul x1 -> x2, other arithmetic: 0.01 us -> 9.09 us  [the longest x1 8.41 us: local(): direction = gradient * (1.0 / jnp.sqrt(totals[0, 0] / (D * D) + 1e-06))]
    div x1 -> x0, other arithmetic: 8.51 us -> none  [local(): direction = gradient / jnp.sqrt(grad_square / (D * D) + 1e-06)]
    unnamed x8, local copies, waits for them, and re-layouts: 11.7 us -> 4.07 us
    reduce_sum x3, other arithmetic: 11.9 us -> 6.03 us  [the longest x1 4 us: local(): error_local = jnp.sum(live_mask * sine * sine)]
    all_gather x0 -> x1, local copies, waits for them, and re-layouts: none -> 3.22 us  [local(): features = lax.all_gather(hidden, 'tensor', axis=1, tiled=True)]
  transfers between devices with their start and end apart: 3 -> 3, of which waited for: 3 -> 3; matrix products, arithmetic and copies ran while one was open for 0% -> 1% of each run, Pallas kernels for 0% -> 0%
where the time goes in v2:
time: 263 us; the launch traced here: 262 us
  waiting for transfers between devices  152 us (58%)
  blocking collectives  30 us (11%)
  Pallas kernels  26.5 us (10%)
  between operations  17.4 us (7%)
  other arithmetic  15.9 us (6%)
  local copies, waits for them, and re-layouts  10.3 us (4%)
  matrix products  10.2 us (4%)
    reduce_scatter x1, waiting for transfers between devices, local(): rotated = lax.psum_scatter(partial, 'dp', scatter_dimension=0, tiled=True)  67.6 us
    all_gather x1, waiting for transfers between devices, local(): features = lax.all_gather(hidden, 'tensor', axis=1, tiled=True)  50.3 us
    all_gather x1, waiting for transfers between devices, local(): slopes = lax.all_gather(error_slope, 'dp', axis=0, tiled=True)  33 us
    all_to_all x1, blocking collectives, local(): lax.all_to_all(features, 'dp', split_axis=1, concat_axis=0, tiled=True)  30 us
    pallas_call x1, Pallas kernels, gradient_call(): pl.pallas_call(functools.partial(gradient_kernel, nd, nt, tile), out_shap...  19.7 us
    dot_general x1, matrix products, local(): jnp.dot(column_blocks, narrow_rotation, preferred_element_type=jnp.float32)  10.2 us
    mul x1, other arithmetic, local(): direction = gradient * (1.0 / jnp.sqrt(totals[0, 0] / (D * D) + 1e-06))  8.41 us
    pallas_call x1, Pallas kernels, token_sum(): pl.pallas_call(functools.partial(token_kernel, nt), out_shape=jax.ShapeDt...  6.87 us
  transfers between devices with their start and end apart: 3, of which 3 were waited for; matrix products, arithmetic and copies ran while one was open for 1% of the time, Pallas kernels for 0%

profile of v2, /device:TPU:0, one launch (start us, length us, event | category | flops | bytes accessed | tf_op | source)
XLA Modules:
  0.0 262.2 jit_solution(11081871443842426183)
XLA Ops:
  7.2 0.0 all-gather.3.cloned.1.call-start
  7.2 0.7 all-gather.3.cloned.1.call-update
  7.9 0.0 reduce-scatter.2.cloned.1.call-start
  7.9 50.3 %all-gather.3.cloned.1.call-done = bf16[128,8192]{1,0:T(8,128)(2,1)} async-done(((bf16[128,2048]{1,0:T(8,128)(2,1)}), bf16[128,8192]{1,0:T(8,128)(2,1)}) %all-gather.3.cloned.1.call-update) | async-done | bytes 2097168 | tf_op jit(solution)/shard_map/all_gather | solution.py:133
  58.2 3.2 %copy.9 = bf16[128,8192]{0,1:T(8,128)(2,1)S(1)} copy(bf16[128,8192]{1,0:T(8,128)(2,1)} %all-gather.3.cloned.1.call-done) | data formatting | bytes 4194304 | tf_op jit(solution)/shard_map/all_gather | solution.py:133
  61.5 30.0 %all_to_all.19 = bf16[128,8,1024]{0,2,1:T(8,128)(2,1)S(1)} all-to-all(bf16[128,8,1024]{0,2,1:T(8,128)(2,1)S(1)} %bitcast.19), channel_id=1, replica_groups=mesh['dp'=8,'tensor'=4] {'dp'}, dimensions={1} | all-to-all | bytes 4194304 | tf_op jit(solution)/shard_map/all_to_all | solution.py:134
  91.5 0.0 copy-start.1
  91.5 1.3 copy-done.1
  92.8 10.2 %fusion = f32[1024,2048]{1,0:T(8,128)} fusion(f32[1024,2048]{1,0:T(8,128)} %param.5, bf16[128,8,1024]{0,2,1:T(8,128)(2,1)S(1)} %all_to_all.19), kind=kOutput, calls=%fused_computation.1 | convolution fusion | flops 4297064448 | bytes 18874368 | tf_op jit(solution)/shard_map/dot_general | solution.py:135
  103.0 0.0 copy-start.3
  103.0 0.0 copy-start.2
  103.0 0.0 reduce-scatter.2.cloned.1.call-update
  103.0 0.0 all-gather.5.cloned.1.call-start
  103.1 0.6 copy-done.3
  103.7 0.1 fusion.9
  103.7 67.6 %reduce-scatter.2.cloned.1.call-done = f32[128,2048]{1,0:T(8,128)} async-done(((f32[1024,2048]{1,0:T(8,128)}), f32[128,2048]{1,0:T(8,128)}) %reduce-scatter.2.cloned.1.call-update) | async-done | bytes 1048592 | tf_op jit(solution)/shard_map/reduce_scatter | solution.py:136
  171.4 0.0 copy-done.2
  171.4 1.4 multiply_reduce_fusion
  172.8 0.6 broadcast_in_dim.36.x_ref
  173.4 6.9 %shard_map.59 = f32[8,128]{1,0:T(8,128)} custom-call(f32[8,128]{1,0:T(8,128)} %broadcast_in_dim.36.x_ref), custom_call_target="tpu_custom_call" | custom-call | tf_op jit(solution)/shard_map/pallas_call | solution.py:53
  180.3 0.7 divide_multiply_fusion
  181.0 4.0 %fusion.5 = (f32[]{:T(128)}, bf16[128,2048]{1,0:T(8,128)(2,1)}) fusion(f32[128]{0:T(128)S(1)} %fusion.9, f32[128]{0:T(128)S(1)} %get-tuple-element.7, f32[128,2048]{1,0:T(8,128)} %reduce-scatter.2.cloned.1.call-done, f32[2048]{0:T(1024)S(1)} %copy-done.2, f32[128]{0:T(128)S(1)} %get-tuple-element.6), kind=kLoop, calls=%fused_computation.9 | loop fusion | flops 9699327 | bytes 1582596 | tf_op jit(solution)/shard_map/reduce_sum | solution.py:149
  185.0 0.0 all-gather.5.cloned.1.call-update
  185.0 0.6 reduce_sum.39
  186.2 1.9 bitcast_bitcast_fusion.h_ref
  188.1 0.7 broadcast_select_fusion.extra_ref
  188.8 33.0 %all-gather.5.cloned.1.call-done.s_ref = bf16[1024,2048]{1,0:T(8,128)(2,1)} async-done(((bf16[128,2048]{1,0:T(8,128)(2,1)}), bf16[1024,2048]{1,0:T(8,128)(2,1)}) %all-gather.5.cloned.1.call-update) | async-done | bytes 4194320 | tf_op jit(solution)/shard_map/all_gather | solution.py:154
  221.8 0.0 copy-start
  221.8 2.2 copy-done
  224.0 19.7 %shard_map.60 = (f32[1024,2048]{1,0:T(8,128)}, f32[8,128]{1,0:T(8,128)S(1)}) custom-call(bf16[1024,1024]{1,0:T(8,128)(2,1)S(1)} %bitcast_bitcast_fusion.h_ref, bf16[1024,2048]{1,0:T(8,128)(2,1)S(1)} %copy-done, f32[8,128]{1,0:T(8,128)S(1)} %broadcast_select_fusion.extra_ref), custom_call_target="tpu_custom_call" | custom-call | tf_op jit(solution)/shard_map/pallas_call | solution.py:96
  243.7 0.5 fusion.10
  246.1 8.4 %broadcast_multiply_fusion = f32[1024,2048]{1,0:T(8,128)} fusion(f32[1024,2048]{1,0:T(8,128)} %get-tuple-element.4, f32[]{:T(128)} %bitcast.4), kind=kLoop, calls=%fused_computation | loop fusion | flops 2097152 | bytes 16777220 | tf_op jit(solution)/shard_map/mul | solution.py:158
  (3 shorter events, 0.0 us)
Async XLA Ops:
  7.2 51.1 %all-gather.3.cloned.1.call-start = ((), (), s32[]{:S(2)}) async-start(), calls=%async_computation.2 | async-start | bytes 2621440 | tf_op jit(solution)/shard_map/all_gather | solution.py:133
  7.9 163.5 %reduce-scatter.2.cloned.1.call-start = ((), (), s32[]{:S(2)}) async-start(), calls=%async_computation.3 | async-start | bytes 9437184 | tf_op jit(solution)/shard_map/reduce_scatter | solution.py:136
  91.5 1.3 copy-start.1
  103.0 0.7 copy-start.3
  103.0 68.4 %copy-start.2 = (f32[2048]{0:T(1024)S(1)}, f32[2048]{0:T(1024)}, u32[]{:S(2)}) copy-start(f32[2048]{0:T(1024)} %param.6) | copy-start | bytes 24580
  103.0 118.8 %all-gather.5.cloned.1.call-start = ((), (), s32[]{:S(2)}) async-start(), calls=%async_computation.4 | async-start | bytes 4718592 | tf_op jit(solution)/shard_map/all_gather | solution.py:154
  221.8 2.2 copy-start
Sparse Core Ops, SparseCore 0:
  9.6 48.6 all-gather.2
  103.2 68.1 reduce-scatter.1
  185.1 36.6 all-gather.4

commit v3 on v2

--- a/solution.py
+++ b/solution.py
@@ -117,6 +117,150 @@
     )(h, s, extra)
 
 
+def forward_kernel(nd, nt, hid_ref, w_ref, h_ref, r_ref, feats, part, mate_in, peer_in,
+                   right_s, right_r, left_s, left_r, sc_s, sc_r, own_sem, mate_s, mate_r, peer_s, peer_r):
+    greet([("dp", nd), ("tensor", nt)])
+    i, j = lax.axis_index("dp"), lax.axis_index("tensor")
+    t, width = hid_ref.shape
+    depth = w_ref.shape[0]
+    per = width // depth
+
+    def rows(k):
+        return h_ref.at[pl.ds(pl.multiple_of(k * t, t), t), :]
+
+    def remote(src, dst, send, recv, target):
+        return pltpu.make_async_remote_copy(
+            src_ref=src, dst_ref=dst, send_sem=send, recv_sem=recv, device_id=target, device_id_type=MESH
+        )
+
+    def along(block, send, recv, to):
+        return remote(feats.at[block], feats.at[block], send, recv, {"tensor": to})
+
+    def spread(block):
+        for h in range(per):
+            dest = block * per + h
+            piece = feats.at[block, :, pl.ds(h * depth, depth)]
+
+            @pl.when(dest != i)
+            def _():
+                remote(piece, rows(i), sc_s.at[dest], sc_r.at[i], {"dp": dest}).start()
+
+            @pl.when(dest == i)
+            def _():
+                pltpu.make_async_copy(piece, rows(i), own_sem.at[0]).start()
+
+    feats[j] = hid_ref[...]
+    for step in range(nt):
+        if step < nt - 1:
+            @pl.when((j - step >= 0) & (j < nt - 1))
+            def _():
+                along(lax.max(j - step, 0), right_s.at[step], right_r.at[step], lax.min(j + 1, nt - 1)).start()
+
+            @pl.when((j + step < nt) & (j > 0))
+            def _():
+                along(lax.min(j + step, nt - 1), left_s.at[step], left_r.at[step], lax.max(j - 1, 0)).start()
+
+        if step == 0:
+            spread(j)
+        if step < nt - 1:
+            @pl.when(j - 1 - step >= 0)
+            def _():
+                block = lax.max(j - 1 - step, 0)
+                along(block, right_s.at[step], right_r.at[step], lax.min(j + 1, nt - 1)).wait_recv()
+                spread(block)
+
+            @pl.when(j + 1 + step < nt)
+            def _():
+                block = lax.min(j + 1 + step, nt - 1)
+                along(block, left_s.at[step], left_r.at[step], lax.max(j - 1, 0)).wait_recv()
+                spread(block)
+
+    chips = nd // 2
+    core, chip = lax.rem(i, 2), i // 2
+    mate = chip * 2 + 1 - core
+    mine = pl.ds(pl.multiple_of(core * t, t), t)
+    other = pl.ds(pl.multiple_of((1 - core) * t, t), t)
+    pltpu.make_async_copy(rows(i), rows(i), own_sem.at[0]).wait()
+
+    def arrive(k):
+        @pl.when(k != i)
+        def _():
+            remote(rows(k), rows(k), sc_s.at[k], sc_r.at[k], {"dp": k}).wait_recv()
+
+    def to_mate(step):
+        return remote(part.at[step, other, :], mate_in.at[step], mate_s.at[step], mate_r.at[step], {"dp": mate})
+
+    def to_peer(step):
+        dest = lax.rem(chip + step + 1, chips) * 2 + core
+        return remote(part.at[step, mine, :], peer_in.at[step], peer_s.at[step], peer_r.at[step], {"dp": dest})
+
+    def join(step):
+        to_mate(step).wait_recv()
+        part[step, mine, :] = part[step, mine, :] + mate_in[step]
+        if step < chips - 1:
+            to_peer(step).start()
+
+    for step in range(chips):
+        q = lax.rem(chip + step + 1, chips)
+        arrive(2 * q)
+        arrive(2 * q + 1)
+        lines = pl.ds(pl.multiple_of(q * 2 * t, 2 * t), 2 * t)
+        part[step] = jnp.dot(h_ref[lines, :], w_ref[...], preferred_element_type=jnp.float32)
+        to_mate(step).start()
+        if step > 0:
+            join(step - 1)
+    join(chips - 1)
+    r_ref[...] = part[chips - 1, mine, :]
+    for step in range(chips - 1):
+        to_peer(step).wait_recv()
+        r_ref[...] += peer_in[step]
+
+    for step in range(chips):
+        to_mate(step).wait_send()
+        if step < chips - 1:
+            to_peer(step).wait_send()
+    for off in range(1, nd):
+        k = lax.rem(i + off, nd)
+        remote(rows(k), rows(k), sc_s.at[k], sc_r.at[k], {"dp": k}).wait_send()
+    for step in range(nt - 1):
+        @pl.when((j - step >= 0) & (j < nt - 1))
+        def _():
+            along(lax.max(j - step, 0), right_s.at[step], right_r.at[step], lax.min(j + 1, nt - 1)).wait_send()
+
+        @pl.when((j + step < nt) & (j > 0))
+        def _():
+            along(lax.min(j + step, nt - 1), left_s.at[step], left_r.at[step], lax.max(j - 1, 0)).wait_send()
+
+
+def forward_call(nd, nt, hidden, w):
+    t, width = hidden.shape
+    depth, columns = w.shape
+    vmem = pl.BlockSpec(memory_space=pltpu.VMEM)
+    dma = pltpu.SemaphoreType.DMA
+    chips = nd // 2
+    return pl.pallas_call(
+        functools.partial(forward_kernel, nd, nt),
+        out_shape=(
+            jax.ShapeDtypeStruct((nd * t, depth), jnp.bfloat16),
+            jax.ShapeDtypeStruct((t, columns), jnp.float32),
+        ),
+        in_specs=[vmem, vmem],
+        out_specs=(vmem, vmem),
+        scratch_shapes=[
+            pltpu.VMEM((nt, t, width), jnp.bfloat16),
+            pltpu.VMEM((chips, 2 * t, columns), jnp.float32),
+            pltpu.VMEM((chips, t, columns), jnp.float32),
+            pltpu.VMEM((chips, t, columns), jnp.float32),
+            dma((nt,)), dma((nt,)), dma((nt,)), dma((nt,)),
+            dma((nd,)), dma((nd,)), dma((1,)),
+            dma((chips,)), dma((chips,)), dma((chips,)), dma((chips,)),
+        ],
+        compiler_params=pltpu.CompilerParams(
+            collective_id=2, has_side_effects=True, vmem_limit_bytes=48 * 1024 * 1024
+        ),
+    )(hidden, w)
+
+
 def sin_cos_pi(turns):
     v = turns - jnp.round(turns)
     x = math.pi * v
@@ -130,10 +274,7 @@
     nd, nt = lax.axis_size("dp"), lax.axis_size("tensor")
     tokens = hidden.shape[0]
     narrow_rotation = rotation.astype(jnp.bfloat16)
-    features = lax.all_gather(hidden, "tensor", axis=1, tiled=True)
-    column_blocks = lax.all_to_all(features, "dp", split_axis=1, concat_axis=0, tiled=True)
-    partial = jnp.dot(column_blocks, narrow_rotation, preferred_element_type=jnp.float32)
-    rotated = lax.psum_scatter(partial, "dp", scatter_dimension=0, tiled=True)
+    column_blocks, rotated = forward_call(nd, nt, hidden, narrow_rotation)
     scaled = rotated * channel_scale[None, :]
     own_square = jnp.sum(scaled * scaled, axis=1)
     token_square = token_sum(nt, jnp.broadcast_to(own_square[None, :], (8, tokens)))[0]

time: 263 us -> 234 us (0.89)
  Pallas kernels: 26.5 us -> 152 us
  waiting for transfers between devices: 152 us -> 37.3 us
  blocking collectives: 30 us -> 0 us
  matrix products: 10.2 us -> 0 us
  other arithmetic: 15.9 us -> 19.6 us
    pallas_call x0 -> x1, Pallas kernels: none -> 114 us  [forward_call(): pl.pallas_call(functools.partial(forward_kernel, nd, nt), out_shape=(jax....]
    reduce_scatter x1 -> x0, waiting for transfers between devices: 67.6 us -> none  [local(): rotated = lax.psum_scatter(partial, 'dp', scatter_dimension=0, tiled=True)]
    all_gather x1 -> x0, waiting for transfers between devices: 50.3 us -> none  [local(): features = lax.all_gather(hidden, 'tensor', axis=1, tiled=True)]
    all_to_all x1 -> x0, blocking collectives: 30 us -> none  [local(): lax.all_to_all(features, 'dp', split_axis=1, concat_axis=0, tiled=True)]
    pallas_call x1, Pallas kernels: 6.87 us -> 18.3 us  [token_sum(): pl.pallas_call(functools.partial(token_kernel, nt), out_shape=jax.ShapeDt...]
    dot_general x1 -> x0, matrix products: 10.2 us -> none  [local(): jnp.dot(column_blocks, narrow_rotation, preferred_element_type=jnp.float32)]
    convert_element_type x0 -> x1, other arithmetic: none -> 6.1 us  [local(): narrow_rotation = rotation.astype(jnp.bfloat16)]
    all_gather x1, waiting for transfers between devices: 33 us -> 37.3 us  [local(): slopes = lax.all_gather(error_slope, 'dp', axis=0, tiled=True)]
  transfers between devices with their start and end apart: 3 -> 1, of which waited for: 3 -> 1; matrix products, arithmetic and copies ran while one was open for 1% -> 2% of each run, Pallas kernels for 0% -> 0%
where the time goes in v3:
time: 234 us
  Pallas kernels  152 us (65%)
  waiting for transfers between devices  37.3 us (16%)
  other arithmetic  19.6 us (8%)
  between operations  17.8 us (8%)
  local copies, waits for them, and re-layouts  7.69 us (3%)
    pallas_call x1, Pallas kernels, forward_call(): pl.pallas_call(functools.partial(forward_kernel, nd, nt), out_shape=(jax....  114 us
    all_gather x1, waiting for transfers between devices, local(): slopes = lax.all_gather(error_slope, 'dp', axis=0, tiled=True)  37.3 us
    pallas_call x1, Pallas kernels, gradient_call(): pl.pallas_call(functools.partial(gradient_kernel, nd, nt, tile), out_shap...  19.7 us
    pallas_call x1, Pallas kernels, token_sum(): pl.pallas_call(functools.partial(token_kernel, nt), out_shape=jax.ShapeDt...  18.3 us
    mul x1, other arithmetic, local(): direction = gradient * (1.0 / jnp.sqrt(totals[0, 0] / (D * D) + 1e-06))  8.41 us
    convert_element_type x1, other arithmetic, local(): narrow_rotation = rotation.astype(jnp.bfloat16)  6.1 us
  transfers between devices with their start and end apart: 1, of which 1 were waited for; matrix products, arithmetic and copies ran while one was open for 2% of the time, Pallas kernels for 0%

profile of v3, /device:TPU:0, one launch (start us, length us, event | category | flops | bytes accessed | tf_op | source)
XLA Modules:
  0.0 234.1 jit_solution(16669728752754650275)
XLA Ops:
  7.2 0.0 copy-start.2
  7.2 0.0 all-gather.2.cloned.1.call-start
  7.2 0.0 copy-start.3
  7.2 0.0 copy-start.4
  7.3 6.1 %convert_element_type.9.w_ref = bf16[1024,2048]{1,0:T(8,128)(2,1)} convert(f32[1024,2048]{1,0:T(8,128)} %param.5) | non-fusion elementwise | flops 2097152 | bytes 12582912 | tf_op jit(solution)/shard_map/convert_element_type | solution.py:276
  13.4 0.0 copy-done.2
  13.4 113.7 %shard_map.59 = (bf16[1024,1024]{1,0:T(8,128)(2,1)S(1)}, f32[128,2048]{1,0:T(8,128)S(1)}) custom-call(bf16[128,2048]{1,0:T(8,128)(2,1)S(1)} %copy-done.2, bf16[1024,2048]{1,0:T(8,128)(2,1)} %convert_element_type.9.w_ref), custom_call_target="tpu_custom_call" | custom-call | tf_op jit(solution)/shard_map/pallas_call | solution.py:241
  127.0 0.0 copy-start.1
  127.0 1.3 copy-done.1
  128.4 0.0 copy-done.3
  128.4 0.2 multiply_reduce_fusion
  128.5 0.6 broadcast_in_dim.36.x_ref
  129.1 18.3 %shard_map.60 = f32[8,128]{1,0:T(8,128)} custom-call(f32[8,128]{1,0:T(8,128)} %broadcast_in_dim.36.x_ref), custom_call_target="tpu_custom_call" | custom-call | tf_op jit(solution)/shard_map/pallas_call | solution.py:53
  147.4 0.0 copy-done.4
  147.5 0.1 fusion.5
  147.5 0.7 divide_multiply_fusion
  148.2 2.8 %fusion.1 = (f32[]{:T(128)}, bf16[128,2048]{1,0:T(8,128)(2,1)}) fusion(f32[128]{0:T(128)S(1)} %fusion.5, f32[128]{0:T(128)S(1)} %get-tuple-element.11, f32[128,2048]{1,0:T(8,128)S(1)} %get-tuple-element.7, f32[2048]{0:T(1024)S(1)} %copy-done.3, f32[128]{0:T(128)S(1)} %get-tuple-element.10), kind=kLoop, calls=%fused_computation.4 | loop fusion | flops 9699327 | bytes 1582596 | tf_op jit(solution)/shard_map/reduce_sum | solution.py:290
  151.0 0.0 all-gather.2.cloned.1.call-update
  151.0 0.6 reduce_sum.39
  152.2 3.0 %copy.7 = bf16[1024,1024]{0,1:T(8,128)(2,1)S(1)} copy(bf16[1024,1024]{1,0:T(8,128)(2,1)} %copy-done.1) | data formatting | bytes 4194304 | tf_op jit(solution)/shard_map/pallas_call | solution.py:241
  155.3 0.7 broadcast_select_fusion.extra_ref
  156.0 37.3 %all-gather.2.cloned.1.call-done.s_ref = bf16[1024,2048]{1,0:T(8,128)(2,1)} async-done(((bf16[128,2048]{1,0:T(8,128)(2,1)}), bf16[1024,2048]{1,0:T(8,128)(2,1)}) %all-gather.2.cloned.1.call-update) | async-done | bytes 4194320 | tf_op jit(solution)/shard_map/all_gather | solution.py:295
  193.3 0.0 copy-start
  193.3 2.2 copy-done
  195.5 19.7 %shard_map.61 = (f32[1024,2048]{1,0:T(8,128)}, f32[8,128]{1,0:T(8,128)S(1)}) custom-call(bf16[1024,1024]{1,0:T(8,128)(2,1)S(1)} %bitcast.6, bf16[1024,2048]{1,0:T(8,128)(2,1)S(1)} %copy-done, f32[8,128]{1,0:T(8,128)S(1)} %broadcast_select_fusion.extra_ref), custom_call_target="tpu_custom_call" | custom-call | tf_op jit(solution)/shard_map/pallas_call | solution.py:96
  215.2 0.5 fusion.6
  217.7 8.4 %broadcast_multiply_fusion = f32[1024,2048]{1,0:T(8,128)} fusion(f32[1024,2048]{1,0:T(8,128)} %get-tuple-element.8, f32[]{:T(128)} %bitcast.2), kind=kLoop, calls=%fused_computation | loop fusion | flops 2097152 | bytes 16777220 | tf_op jit(solution)/shard_map/mul | solution.py:299
  (3 shorter events, 0.0 us)
Async XLA Ops:
  7.2 6.2 %copy-start.2 = (bf16[128,2048]{1,0:T(8,128)(2,1)S(1)}, bf16[128,2048]{1,0:T(8,128)(2,1)}, u32[]{:S(2)}) copy-start(bf16[128,2048]{1,0:T(8,128)(2,1)} %hid_ref.1) | copy-start | bytes 1572868
  7.2 186.2 %all-gather.2.cloned.1.call-start = ((), (), s32[]{:S(2)}) async-start(), calls=%async_computation | async-start | bytes 4718592 | tf_op jit(solution)/shard_map/all_gather | solution.py:295
  7.2 121.1 %copy-start.3 = (f32[2048]{0:T(1024)S(1)}, f32[2048]{0:T(1024)}, u32[]{:S(2)}) copy-start(f32[2048]{0:T(1024)} %param.6) | copy-start | bytes 24580
  7.2 140.2 %copy-start.4 = (s32[2]{0:T(128)S(1)}, s32[2]{0:T(128)}, u32[]{:S(2)}) copy-start(s32[2]{0:T(128)} %param.7) | copy-start | bytes 28
  127.0 1.3 copy-start.1
  193.3 2.2 copy-start
Sparse Core Ops, SparseCore 0:
  151.1 42.1 all-gather.1

commit v4 on v3

--- a/solution.py
+++ b/solution.py
@@ -64,13 +64,49 @@
     )(x)
 
 
-def gradient_kernel(nd, nt, tile, h_ref, s_ref, extra_ref, g_ref, o_ref, buf, out_sem, tslots, dslots, ts, tr, ds, dr):
+def gradient_kernel(nd, nt, tile, h_ref, own_ref, extra_ref, g_ref, o_ref, s_ref, buf, out_sem, tslots, dslots,
+                    ts, tr, ds, dr, peer_s, peer_r, mate_s, mate_r):
     greet([("dp", nd), ("tensor", nt)])
+    i = lax.axis_index("dp")
+    core, chip, chips = lax.rem(i, 2), i // 2, nd // 2
+    mate = chip * 2 + 1 - core
+    t = own_ref.shape[0]
     rows, columns = g_ref.shape
+    half = columns // 2
+
+    def place(k, part):
+        return s_ref.at[pl.ds(pl.multiple_of(k * t, t), t), pl.ds(part * half, half)]
+
+    def remote(src, send, recv, to):
+        return pltpu.make_async_remote_copy(
+            src_ref=src, dst_ref=src, send_sem=send, recv_sem=recv, device_id={"dp": to}, device_id_type=MESH
+        )
+
+    def to_peer(part, step):
+        dest = lax.rem(chip + step, chips) * 2 + core
+        return remote(place(i, part), peer_s.at[part, step], peer_r.at[part, step], dest)
+
+    def to_mate(part, step):
+        source = lax.rem(chip - step + chips, chips) * 2 + core
+        return remote(place(source, part), mate_s.at[part, step], mate_r.at[part, step], mate)
+
+    s_ref[pl.ds(pl.multiple_of(i * t, t), t), :] = own_ref[...]
+    for part in range(2):
+        for step in range(1, chips):
+            to_peer(part, step).start()
+        to_mate(part, 0).start()
+
     steps = columns // tile
     square = jnp.zeros((8, tile), jnp.float32)
     copies = []
     for step in range(steps):
+        if step % (steps // 2) == 0:
+            part = step // (steps // 2)
+            for hop in range(1, chips):
+                to_peer(part, hop).wait_recv()
+                to_mate(part, hop).start()
+            for hop in range(chips):
+                to_mate(part, hop).wait_recv()
         slot = step % 2
         if step >= 2:
             copies[step - 2].wait()
@@ -86,10 +122,15 @@
     o_ref[...] = all_sum("dp", nd, dslots, ds, dr, value)
     for copy in copies[-2:]:
         copy.wait()
-
-
-def gradient_call(nd, nt, h, s, extra):
-    rows, columns = h.shape[0], s.shape[1]
+    for part in range(2):
+        to_mate(part, 0).wait_send()
+        for hop in range(1, chips):
+            to_peer(part, hop).wait_send()
+            to_mate(part, hop).wait_send()
+
+
+def gradient_call(nd, nt, h, own, extra):
+    rows, columns = h.shape[0], own.shape[1]
     tile = 256
     vmem = pl.BlockSpec(memory_space=pltpu.VMEM)
     dma = pltpu.SemaphoreType.DMA
@@ -102,6 +143,7 @@
         in_specs=[vmem, vmem, vmem],
         out_specs=(pl.BlockSpec(memory_space=pl.ANY), vmem),
         scratch_shapes=[
+            pltpu.VMEM((nd * own.shape[0], columns), jnp.bfloat16),
             pltpu.VMEM((2, rows, tile), jnp.float32),
             dma((2,)),
             pltpu.VMEM((nt, 8, 128), jnp.float32),
@@ -110,11 +152,15 @@
             dma((nt,)),
             dma((nd,)),
             dma((nd,)),
+            dma((2, nd // 2)),
+            dma((2, nd // 2)),
+            dma((2, nd // 2)),
+            dma((2, nd // 2)),
         ],
         compiler_params=pltpu.CompilerParams(
             collective_id=1, has_side_effects=True, vmem_limit_bytes=40 * 1024 * 1024
         ),
-    )(h, s, extra)
+    )(h, own, extra)
 
 
 def forward_kernel(nd, nt, hid_ref, w_ref, h_ref, r_ref, feats, part, mate_in, peer_in,
@@ -292,10 +338,9 @@
     error_slope = (
         live_mask * (math.pi / step_size) * (2.0 * sine * cosine) * channel_scale[None, :]
     ).astype(jnp.bfloat16)
-    slopes = lax.all_gather(error_slope, "dp", axis=0, tiled=True)
     row = lax.broadcasted_iota(jnp.int32, (8, 128), 0)
     extra = jnp.where(row == 1, error_local, jnp.where(row == 2, count_local, 0.0))
-    gradient, totals = gradient_call(nd, nt, column_blocks.T, slopes, extra)
+    gradient, totals = gradient_call(nd, nt, column_blocks.T, error_slope, extra)
     direction = gradient * (1.0 / jnp.sqrt(totals[0, 0] / (D * D) + 1e-06))
     loss = totals[1, 0] / (D * totals[2, 0])
     return (direction, loss)

time: 234 us -> 205 us (0.88)
  waiting for transfers between devices: 37.3 us -> 0 us
  Pallas kernels: 152 us -> 179 us
  between operations: 17.8 us -> 4.53 us
  other arithmetic: 19.6 us -> 15.9 us
    all_gather x1 -> x0, waiting for transfers between devices: 37.3 us -> none  [local(): slopes = lax.all_gather(error_slope, 'dp', axis=0, tiled=True)]
    pallas_call x1, Pallas kernels: 19.7 us -> 46.7 us  [gradient_call(): pl.pallas_call(functools.partial(gradient_kernel, nd, nt, tile), out_shap...]
    mul x1, other arithmetic: 8.41 us -> 4.24 us  [local(): direction = gradient * (1.0 / jnp.sqrt(totals[0, 0] / (D * D) + 1e-06))]
  transfers between devices with their start and end apart: 1 -> 0, of which waited for: 1 -> 0; matrix products, arithmetic and copies ran while one was open for 2% -> 0% of each run, Pallas kernels for 0% -> 0%
where the time goes in v4:
time: 205 us; the launch traced here: 204 us
  Pallas kernels  179 us (87%)
  other arithmetic  15.9 us (8%)
  local copies, waits for them, and re-layouts  5.38 us (3%)
  between operations  4.53 us (2%)
    pallas_call x1, Pallas kernels, forward_call(): pl.pallas_call(functools.partial(forward_kernel, nd, nt), out_shape=(jax....  114 us
    pallas_call x1, Pallas kernels, gradient_call(): pl.pallas_call(functools.partial(gradient_kernel, nd, nt, tile), out_shap...  46.7 us
    pallas_call x1, Pallas kernels, token_sum(): pl.pallas_call(functools.partial(token_kernel, nt), out_shape=jax.ShapeDt...  18.2 us
    convert_element_type x1, other arithmetic, local(): narrow_rotation = rotation.astype(jnp.bfloat16)  6.06 us
    mul x1, other arithmetic, local(): direction = gradient * (1.0 / jnp.sqrt(totals[0, 0] / (D * D) + 1e-06))  4.24 us

profile of v4, /device:TPU:0, one launch (start us, length us, event | category | flops | bytes accessed | tf_op | source)
XLA Modules:
  0.0 204.5 jit_solution(15676506371639071345)
XLA Ops:
  0.6 0.0 copy-start.1
  0.6 1.4 reduce_sum.39
  2.7 0.7 fusion.5
  3.4 0.0 copy-start.2
  3.4 6.1 %convert_element_type.9.w_ref = bf16[1024,2048]{1,0:T(8,128)(2,1)} convert(f32[1024,2048]{1,0:T(8,128)} %param.5) | non-fusion elementwise | flops 2097152 | bytes 12582912 | tf_op jit(solution)/shard_map/convert_element_type | solution.py:322
  9.5 0.0 copy-done.1
  9.5 113.7 %shard_map.59 = (bf16[1024,1024]{1,0:T(8,128)(2,1)S(1)}, f32[128,2048]{1,0:T(8,128)S(1)}) custom-call(bf16[128,2048]{1,0:T(8,128)(2,1)S(1)} %copy-done.1, bf16[1024,2048]{1,0:T(8,128)(2,1)} %convert_element_type.9.w_ref), custom_call_target="tpu_custom_call" | custom-call | tf_op jit(solution)/shard_map/pallas_call | solution.py:287
  123.2 0.0 copy-start
  123.2 1.3 copy-done
  124.5 2.9 %copy.7 = bf16[1024,1024]{0,1:T(8,128)(2,1)S(1)} copy(bf16[1024,1024]{1,0:T(8,128)(2,1)} %copy-done) | data formatting | bytes 4194304 | tf_op jit(solution)/shard_map/pallas_call | solution.py:287
  127.4 0.0 copy-done.2
  127.4 0.2 multiply_reduce_fusion
  127.6 0.6 broadcast_in_dim.36.x_ref
  128.2 18.2 %shard_map.60 = f32[8,128]{1,0:T(8,128)} custom-call(f32[8,128]{1,0:T(8,128)} %broadcast_in_dim.36.x_ref), custom_call_target="tpu_custom_call" | custom-call | tf_op jit(solution)/shard_map/pallas_call | solution.py:53
  146.5 0.7 divide_multiply_fusion
  147.2 1.9 fusion.1
  149.0 0.7 broadcast_select_fusion.extra_ref
  149.7 46.7 %shard_map.61 = (f32[1024,2048]{1,0:T(8,128)S(1)}, f32[8,128]{1,0:T(8,128)S(1)}) custom-call(bf16[1024,1024]{1,0:T(8,128)(2,1)S(1)} %bitcast.6, bf16[128,2048]{1,0:T(8,128)(2,1)S(1)} %get-tuple-element.13.own_ref, f32[8,128]{1,0:T(8,128)S(1)} %broadcast_select_fusion.extra_ref), custom_call_target="tpu_custom_call" | custom-call | tf_op jit(solution)/shard_map/pallas_call | solution.py:137
  196.4 0.6 fusion.6
  199.1 4.2 %broadcast_multiply_fusion = f32[1024,2048]{1,0:T(8,128)} fusion(f32[1024,2048]{1,0:T(8,128)S(1)} %get-tuple-element.8, f32[]{:T(128)} %bitcast.2), kind=kLoop, calls=%fused_computation | loop fusion | flops 2097152 | bytes 16777220 | tf_op jit(solution)/shard_map/mul | solution.py:344
  (3 shorter events, 0.0 us)
Async XLA Ops:
  0.6 8.9 %copy-start.1 = (bf16[128,2048]{1,0:T(8,128)(2,1)S(1)}, bf16[128,2048]{1,0:T(8,128)(2,1)}, u32[]{:S(2)}) copy-start(bf16[128,2048]{1,0:T(8,128)(2,1)} %hid_ref.1) | copy-start | bytes 1572868
  3.4 124.0 %copy-start.2 = (f32[2048]{0:T(1024)S(1)}, f32[2048]{0:T(1024)}, u32[]{:S(2)}) copy-start(f32[2048]{0:T(1024)} %param.6) | copy-start | bytes 24580
  123.2 1.3 copy-start
